TPU v7x, 1024 devices: a whole 4x4x32 slice. The times are simulated.
1024 devices in a mesh: row: 16 (over z_hi, y, core), col: 64 (over z_lo, x).
Axes of the slice: x: 4, y: 4, z: 32 (z_hi: 2, z_lo: 16; z = z_hi * 16 + z_lo), core: 2. Of those that a mesh axis runs over, the one named last changes fastest.
Arguments:
- amplitudes: float32 [320, 45056], P('col', 'row'), may hold values from -6 to 6
- integrals: float32 [45056, 16384], P('row', 'col'), may hold values from -0.02734375 to 0.02734375
- direct_terms: float32 [320, 16384], P('row', 'col'), may hold values from -4 to 4
- occ_energy: float32 [320], P('row'), may hold values from -4 to -1
- virt_energy: float32 [16384], P('col'), may hold values from 0.5 to 4
Outputs:
- updated: float32 [320, 16384], P('row', 'col')
All inputs are finite; a program needn't handle non-finite values.
Results may differ from a plain program's by a relative error of at most 0.000056.
Values sent between devices are 32-bit elements; how exact they have to be, the bound alone decides.
A program may use at most 32 MiB of HBM per device.

v0:
```python
import jax
import jax.numpy as jnp
from jax import lax
from jax.sharding import PartitionSpec as P


def per_device(amplitudes, integrals, direct_terms, occ_energy, virt_energy):
    blocked = lax.all_to_all(amplitudes, "col", split_axis=1, concat_axis=0, tiled=True)
    panel = lax.all_gather(blocked, "col", axis=1, tiled=True)
    partial_value = jnp.dot(
        panel, integrals, precision=lax.Precision.HIGHEST, preferred_element_type=jnp.float32
    )
    ladder = lax.psum_scatter(partial_value, "row", scatter_dimension=0, tiled=True)
    denominator = occ_energy[:, None] - virt_energy[None, :]
    return (0.5 * ladder + direct_terms) / denominator


def solution(mesh):
    in_specs = (P("col", "row"), P("row", "col"), P("row", "col"), P("row"), P("col"))
    out_specs = P("row", "col")
    return jax.shard_map(
        per_device, mesh=mesh, in_specs=in_specs, out_specs=out_specs, check_vma=False
    )
```

profile of v0, /device:TPU:25, one launch (start us, length us, event | category | flops | bytes accessed | tf_op | source)
XLA Modules:
  0.0 922.7 jit_solution(13580579837350734056)
XLA Ops:
  6.5 0.0 copy-start
  6.5 0.0 all-gather.3.cloned.1.call-start
  6.5 1.2 all_to_all.14
  7.8 0.1 copy.11
  7.9 0.2 reshape.8
  8.1 49.9 %all_to_all.19 = f32[64,1,220]{2,1,0:T(1,128)S(1)} all-to-all(f32[64,1,220]{2,1,0:T(1,128)S(1)} %reshape.8), channel_id=1, replica_groups=mesh['row'=16,'col'=64] {'col'}, dimensions={0} | all-to-all | bytes 112640 | tf_op jit(solution)/shard_map/all_to_all | solution.py:8
  58.0 0.5 broadcast.2
  58.5 0.8 reduce
  59.3 0.1 reshape.9
  59.5 0.8 copy.9
  60.2 0.0 all-gather.3.cloned.1.call-update
  60.2 660.9 %all-gather.3.cloned.1.call-done = f32[64,44,320]{2,1,0:T(8,128)} async-done(((f32[1,44,320]{2,1,0:T(8,128)}), f32[64,44,320]{2,1,0:T(8,128)}) %all-gather.3.cloned.1.call-update) | async-done | bytes 3604496 | tf_op jit(solution)/shard_map/all_gather | solution.py:9
  721.1 5.0 reshape.6
  726.1 0.0 copy-done
  726.1 0.0 copy-start.1
  726.1 0.0 copy-start.2
  726.2 0.0 copy-start.3
  726.2 9.2 fusion.3
  735.4 147.7 %fusion = f32[24,256]{1,0:T(8,128)S(1)} fusion(f32[320,256]{1,0:T(8,128)S(1)} %fusion.3), kind=kCustom, calls=%all-reduce-scatter | all-reduce-scatter fusion | flops 98305 | bytes 356352
  883.0 24.6 %collective-permute-start = (f32[24,256]{1,0:T(8,128)S(1)}, f32[24,256]{1,0:T(8,128)S(1)}, u32[]{:S(2)}, u32[]{:S(2)}) collective-permute-start(f32[24,256]{1,0:T(8,128)S(1)} %fusion), channel_id=1, source_target_pairs={{0,64},{64,128},{128,192},{192,256},{256,320},{320,384},{384,448},... | collective-permute-start | bytes 73736
  907.7 1.9 collective-permute-start.1
  909.6 1.9 collective-permute-start.2
  911.6 1.3 dynamic-slice.4
  913.5 1.2 collective-permute-done.2
  914.7 0.0 collective-permute-done
  914.7 0.0 collective-permute-done.1
  914.7 0.4 concatenate
  915.1 0.0 copy-done.1
  915.1 0.0 copy-done.2
  915.1 0.0 copy-done.3
  915.1 0.7 fusion.2
  (3 shorter events, 0.0 us)
Async XLA Ops:
  6.5 719.6 %copy-start = (f32[2816,256]{1,0:T(8,128)S(1)}, f32[2816,256]{1,0:T(8,128)}, u32[]{:S(2)}) copy-start(f32[2816,256]{1,0:T(8,128)} %param.6) | copy-start | bytes 8650756
  6.5 714.6 %all-gather.3.cloned.1.call-start = ((), (), s32[]{:S(2)}) async-start(), calls=%async_computation.1 | async-start | bytes 4792320 | tf_op jit(solution)/shard_map/all_gather | solution.py:9
  726.1 189.0 %copy-start.1 = (f32[20,256]{1,0:T(8,128)S(1)}, f32[20,256]{1,0:T(8,128)}, u32[]{:S(2)}) copy-start(f32[20,256]{1,0:T(8,128)} %param.7) | copy-start | bytes 61444
  726.1 189.0 %copy-start.2 = (f32[256]{0:T(256)S(1)}, f32[256]{0:T(256)}, u32[]{:S(2)}) copy-start(f32[256]{0:T(256)} %param.9) | copy-start | bytes 3076
  726.2 189.0 %copy-start.3 = (f32[20]{0:T(128)S(1)}, f32[20]{0:T(128)}, u32[]{:S(2)}) copy-start(f32[20]{0:T(128)} %param.8) | copy-start | bytes 244
  883.0 31.7 %collective-permute-start = (f32[24,256]{1,0:T(8,128)S(1)}, f32[24,256]{1,0:T(8,128)S(1)}, u32[]{:S(2)}, u32[]{:S(2)}) collective-permute-start(f32[24,256]{1,0:T(8,128)S(1)} %fusion), channel_id=1, source_target_pairs={{0,64},{64,128},{128,192},{192,256},{256,320},{320,384},{384,448},... | collective-permute-start | bytes 73736
  907.7 7.0 collective-permute-start.1
  909.6 5.1 collective-permute-start.2
Sparse Core Ops, SparseCore 0:
  60.4 660.7 all-gather.2
where the time goes:
time: 927 us; the launch traced here: 923 us
  waiting for transfers between devices  662 us (71%)
  blocking collectives  198 us (21%)
  starting transfers between devices  28.5 us (3%)
  between operations  14.2 us (2%)
  local copies, waits for them, and re-layouts  9.66 us (1%)
    all_gather x1, waiting for transfers between devices, per_device(): panel = lax.all_gather(blocked, 'col', axis=1, tiled=True)  661 us
    unnamed x1, blocking collectives  148 us
    all_to_all x1, blocking collectives, per_device(): lax.all_to_all(amplitudes, 'col', split_axis=1, concat_axis=0, tiled=True)  49.9 us
    unnamed x3, starting transfers between devices  28.5 us
  transfers between devices with their start and end apart: 4, of which 2 were waited for; matrix products, arithmetic and copies ran while one was open for 0% of the time, Pallas kernels for 0%

commit v1 on v0

v1 whole, which is shorter than its diff:
```python
import functools

import jax
import jax.numpy as jnp
from jax import lax
from jax.experimental import pallas as pl
from jax.experimental.pallas import tpu as pltpu
from jax.sharding import PartitionSpec as P

MESH = pl.DeviceIdType.MESH
NX = 4
NZ = 16
NR = 5
LANES = 128
PEERS = 8


def kernel(n_chunks, amp_ref, b_hbm, out_ref, own, slabs, b_raw, b_hi, b_lo, lhs, part, part_in, cross, cross_in,
           b_sem, z_send, z_recv, x_send, x_recv, f_send, f_recv, p_send, p_recv, c_send, c_recv):
    rows = own.shape[0]
    half = rows // 2
    row = lax.axis_index("row")
    col = lax.axis_index("col")
    x, z = lax.rem(col, NX), col // NX
    zh, me8 = row // PEERS, lax.rem(row, PEERS)
    right = z * NX + lax.rem(x + 1, NX)
    left = z * NX + lax.rem(x + NX - 1, NX)
    x_left, x_right, x_far = lax.rem(x + 3, NX), lax.rem(x + 1, NX), lax.rem(x + 2, NX)
    partner = (1 - zh) * PEERS + me8

    b_copy = pltpu.make_async_copy(b_hbm, b_raw, b_sem)
    b_copy.start()

    barrier = pltpu.get_barrier_semaphore()

    def greet(r, c):
        pl.semaphore_signal(barrier, inc=1, device_id={"row": r, "col": c}, device_id_type=MESH)

    greet(row, left)
    greet(row, right)
    for d in range(1, PEERS):
        greet(zh * PEERS + lax.rem(me8 + d, PEERS), col)
    greet(partner, col)

    @pl.when(z > 0)
    def _():
        greet(row, col - NX)

    @pl.when(z < NZ - 1)
    def _():
        greet(row, col + NX)

    for k in range(n_chunks):
        own[k * NR : (k + 1) * NR, :] = amp_ref[:, k * LANES : (k + 1) * LANES]
    if n_chunks * NR < rows:
        own[n_chunks * NR :, :] = jnp.zeros((rows - n_chunks * NR, LANES), jnp.float32)
    slabs[z, pl.ds(pl.multiple_of(x * rows, 8), rows), :] = own[...]

    ends = jnp.where(z > 0, 1, 0) + jnp.where(z < NZ - 1, 1, 0)
    pl.semaphore_wait(barrier, 2 + PEERS + ends)

    def piece(zs, xs, p):
        return slabs.at[zs, pl.ds(pl.multiple_of(xs * rows + p * half, 8), half), :]

    def z_copy(zs, p, up):
        to = jnp.minimum(col + NX, NZ * NX - 1) if up else jnp.maximum(col - NX, 0)
        ref = piece(zs, x, p)
        return pltpu.make_async_remote_copy(ref, ref, z_send.at[up, zs, p], z_recv.at[zs, p],
                                            device_id={"row": row, "col": to}, device_id_type=MESH)

    def x_copy(zs, p, to_right):
        ref = piece(zs, x, p)
        return pltpu.make_async_remote_copy(ref, ref, x_send.at[to_right, zs, p], x_recv.at[to_right, zs, p],
                                            device_id={"row": row, "col": right if to_right else left},
                                            device_id_type=MESH)

    def x_arrival(zs, p, to_right):
        ref = piece(zs, x_left if to_right else x_right, p)
        return pltpu.make_async_copy(ref, ref, x_recv.at[to_right, zs, p])

    def f_copy(zs, to_right):
        ref = piece(zs, x_left if to_right else x_right, 1 - to_right)
        return pltpu.make_async_remote_copy(ref, ref, f_send.at[to_right, zs], f_recv.at[to_right, zs],
                                            device_id={"row": row, "col": right if to_right else left},
                                            device_id_type=MESH)

    def f_arrival(zs, to_right):
        ref = piece(zs, x_far, 1 - to_right)
        return pltpu.make_async_copy(ref, ref, f_recv.at[to_right, zs])

    def p_copy(zs):
        to = zh * PEERS + lax.rem(zs, PEERS)
        return pltpu.make_async_remote_copy(part.at[zs], part_in.at[zs // PEERS, me8], p_send.at[zs],
                                            p_recv.at[zs // PEERS, me8],
                                            device_id={"row": to, "col": col}, device_id_type=MESH)

    pairs = jnp.minimum(z, NZ - 1 - z)

    def order(n):
        near = (n + 1) // 2
        near = jnp.where(lax.rem(n, 2) == 1, z - near, z + near)
        far = jnp.where(z < NZ // 2, z + n - pairs, z - n + pairs)
        return jnp.where(n <= 2 * pairs, near, far)

    def z_start(zs, p, up):
        @pl.when((z < NZ - 1) if up else (z > 0))
        def _():
            z_copy(zs, p, up).start()

    def z_step(t):
        for p in range(2):
            @pl.when(z - t >= 0)
            def _():
                z_copy(z - t, p, 1).wait_recv()
                z_start(z - t, p, 1)

            @pl.when(z + t < NZ)
            def _():
                z_copy(z + t, p, 0).wait_recv()
                z_start(z + t, p, 0)

    def x_start(zs):
        x_copy(zs, 0, 1).start()
        x_copy(zs, 1, 0).start()
        x_copy(zs, 1, 1).start()
        x_copy(zs, 0, 0).start()

    def x_forward(zs):
        x_arrival(zs, 0, 1).wait()
        f_copy(zs, 1).start()
        x_arrival(zs, 1, 0).wait()
        f_copy(zs, 0).start()

    def finish(zs):
        x_arrival(zs, 1, 1).wait()
        x_arrival(zs, 0, 0).wait()
        f_arrival(zs, 1).wait()
        f_arrival(zs, 0).wait()
        for q in range(NX // 2):
            for k in range(n_chunks):
                v = jnp.concatenate(
                    [slabs[zs, (2 * q + i) * rows + k * NR : (2 * q + i) * rows + k * NR + 8, :] for i in range(2)],
                    axis=0)
                hi = v.astype(jnp.bfloat16)
                lo = (v - hi.astype(jnp.float32)).astype(jnp.bfloat16)
                lhs[16 * q : 16 * q + 16, k * LANES : (k + 1) * LANES] = hi
                lhs[32 + 16 * q : 48 + 16 * q, k * LANES : (k + 1) * LANES] = lo
        both = jnp.dot(lhs[...], b_hi[...], preferred_element_type=jnp.float32)
        cross_term = jnp.dot(lhs[:32, :], b_lo[...], preferred_element_type=jnp.float32)
        part[zs] = both[:32] + (both[32:] + cross_term)

        @pl.when(lax.rem(zs, PEERS) != me8)
        def _():
            p_copy(zs).start()

    for p in range(2):
        z_start(z, p, 1)
        z_start(z, p, 0)
    x_start(z)

    b_copy.wait()
    depth = b_raw.shape[0]

    @pl.loop(0, depth // 256)
    def _(i):
        at = pl.ds(pl.multiple_of(i * 256, 256), 256)
        v = b_raw[at, :]
        hi = v.astype(jnp.bfloat16)
        b_hi[at, :] = hi
        b_lo[at, :] = (v - hi.astype(jnp.float32)).astype(jnp.bfloat16)

    @pl.loop(1, NZ + 2)
    def _(t):
        z_step(t)

        @pl.when(t < NZ)
        def _():
            x_start(order(t))

        @pl.when(t < NZ + 1)
        def _():
            x_forward(order(t - 1))

        @pl.when(t >= 2)
        def _():
            finish(order(t - 2))

    def total(h):
        s = part[h * PEERS + me8]
        for d in range(1, PEERS):
            q = lax.rem(me8 + d, PEERS)
            ref = part_in.at[h, q]
            pltpu.make_async_copy(ref, ref, p_recv.at[h, q]).wait()
            s = s + part_in[h, q]
        return jnp.concatenate([s[8 * i : 8 * i + NR, :] for i in range(NX)], axis=0)

    cross[...] = total(1 - zh)
    c_copy = pltpu.make_async_remote_copy(cross, cross_in, c_send, c_recv,
                                          device_id={"row": partner, "col": col}, device_id_type=MESH)
    c_copy.start()
    mine = total(zh)
    c_copy.wait_recv()
    out_ref[...] = mine + cross_in[...]
    c_copy.wait_send()

    @pl.loop(0, NZ)
    def _(zs):
        for p in range(2):
            @pl.when((z < NZ - 1) & (zs <= z))
            def _():
                z_copy(zs, p, 1).wait_send()

            @pl.when((z > 0) & (zs >= z))
            def _():
                z_copy(zs, p, 0).wait_send()

            for to_right in range(2):
                x_copy(zs, p, to_right).wait_send()
        for to_right in range(2):
            f_copy(zs, to_right).wait_send()

        @pl.when(lax.rem(zs, PEERS) != me8)
        def _():
            p_copy(zs).wait_send()


def ladder_rows(amplitudes, integrals):
    depth, width = integrals.shape
    n_chunks = depth // LANES
    rows = -(-n_chunks * NR // 16) * 16
    f32, bf16 = jnp.float32, jnp.bfloat16
    dma = pltpu.SemaphoreType.DMA
    return pl.pallas_call(
        functools.partial(kernel, n_chunks),
        out_shape=jax.ShapeDtypeStruct((NX * NR, width), f32),
        in_specs=[pl.BlockSpec(memory_space=pltpu.VMEM), pl.BlockSpec(memory_space=pl.ANY)],
        out_specs=pl.BlockSpec(memory_space=pltpu.VMEM),
        scratch_shapes=[
            pltpu.VMEM((rows, LANES), f32),
            pltpu.VMEM((NZ, NX * rows + 8, LANES), f32),
            pltpu.VMEM((depth, width), f32),
            pltpu.VMEM((depth, width), bf16),
            pltpu.VMEM((depth, width), bf16),
            pltpu.VMEM((64, depth), bf16),
            pltpu.VMEM((NZ, 32, width), f32),
            pltpu.VMEM((2, PEERS, 32, width), f32),
            pltpu.VMEM((NX * NR, width), f32),
            pltpu.VMEM((NX * NR, width), f32),
            dma,
            dma((2, NZ, 2)),
            dma((NZ, 2)),
            dma((2, NZ, 2)),
            dma((2, NZ, 2)),
            dma((2, NZ)),
            dma((2, NZ)),
            dma((NZ,)),
            dma((2, PEERS)),
            dma,
            dma,
        ],
        compiler_params=pltpu.CompilerParams(
            collective_id=0, has_side_effects=True, vmem_limit_bytes=40 * 1024 * 1024),
        cost_estimate=pl.CostEstimate(
            flops=6 * 512 * depth * width, bytes_accessed=4 * depth * width, transcendentals=0),
        name="ladder",
    )(amplitudes, integrals)


def per_device(amplitudes, integrals, direct_terms, occ_energy, virt_energy):
    ladder = ladder_rows(amplitudes, integrals)
    denominator = occ_energy[:, None] - virt_energy[None, :]
    return (0.5 * ladder + direct_terms) / denominator


def solution(mesh):
    in_specs = (P("col", "row"), P("row", "col"), P("row", "col"), P("row"), P("col"))
    out_specs = P("row", "col")
    return jax.shard_map(
        per_device, mesh=mesh, in_specs=in_specs, out_specs=out_specs, check_vma=False
    )
```

time: 927 us -> 98.6 us (0.11)
  the two profiles are of different devices: /device:TPU:25 before, /device:TPU:8 now
where the time goes in v1:
time: 98.6 us; the launch traced here: 98.3 us
  Pallas kernels  94.9 us (96%)
  local copies, waits for them, and re-layouts  2.71 us (3%)
    pallas_call x1, Pallas kernels, ladder_rows(): pl.pallas_call(functools.partial(kernel, n_chunks), out_shape=jax.ShapeDt...  94.9 us
    unnamed x10, local copies, waits for them, and re-layouts  2.71 us

profile of v1, /device:TPU:8, one launch (start us, length us, event | category | flops | bytes accessed | tf_op | source)
XLA Modules:
  0.0 98.3 jit_solution(16340615552618454990)
XLA Ops:
  0.0 0.0 copy-start
  0.0 1.8 %copy-done = f32[2816,256]{1,0:T(8,128)S(1)} copy-done((f32[2816,256]{1,0:T(8,128)S(1)}, f32[2816,256]{1,0:T(8,128)}, u32[]{:S(2)}) %copy-start) | copy-done | bytes 2883608
  1.8 0.0 copy-start.1
  1.8 0.9 copy-done.1
  2.7 0.0 copy-start.2
  2.7 0.0 copy-start.3
  2.7 0.0 copy-start.4
  2.7 94.9 %ladder.1 = f32[20,256]{1,0:T(8,128)S(1)} custom-call(f32[5,2816]{1,0:T(8,128)S(1)} %copy-done.1, f32[2816,256]{1,0:T(8,128)S(1)} %copy-done), custom_call_target="tpu_custom_call" | custom-call | flops 2214592512 | bytes 2883584 | tf_op jit(solution)/shard_map/ladder/pallas_call | solution.py:233
  97.6 0.0 copy-done.2
  97.6 0.0 copy-done.3
  97.6 0.0 copy-done.4
  97.6 0.7 subtract_divide_fusion
Async XLA Ops:
  0.0 1.8 %copy-start = (f32[2816,256]{1,0:T(8,128)S(1)}, f32[2816,256]{1,0:T(8,128)}, u32[]{:S(2)}) copy-start(f32[2816,256]{1,0:T(8,128)} %b_hbm.1) | copy-start | bytes 8650756
  1.8 0.9 copy-start.1
  2.7 94.9 %copy-start.2 = (f32[20,256]{1,0:T(8,128)S(1)}, f32[20,256]{1,0:T(8,128)}, u32[]{:S(2)}) copy-start(f32[20,256]{1,0:T(8,128)} %param.7) | copy-start | bytes 61444
  2.7 94.9 %copy-start.3 = (f32[256]{0:T(256)S(1)}, f32[256]{0:T(256)}, u32[]{:S(2)}) copy-start(f32[256]{0:T(256)} %param.9) | copy-start | bytes 3076
  2.7 94.9 %copy-start.4 = (f32[20]{0:T(128)S(1)}, f32[20]{0:T(128)}, u32[]{:S(2)}) copy-start(f32[20]{0:T(128)} %param.8) | copy-start | bytes 244

commit v2 on v1

--- a/solution.py
+++ b/solution.py
@@ -16,7 +16,7 @@
 
 
 def kernel(n_chunks, amp_ref, b_hbm, out_ref, own, slabs, b_raw, b_hi, b_lo, lhs, part, part_in, cross, cross_in,
-           b_sem, z_send, z_recv, x_send, x_recv, f_send, f_recv, p_send, p_recv, c_send, c_recv):
+           b_sem, z_send, z_recv, x_send, x_recv, f_send, f_recv, p_send, p_recv, c_send, c_recv, here_sem):
     rows = own.shape[0]
     half = rows // 2
     row = lax.axis_index("row")
@@ -26,11 +26,11 @@
     right = z * NX + lax.rem(x + 1, NX)
     left = z * NX + lax.rem(x + NX - 1, NX)
     x_left, x_right, x_far = lax.rem(x + 3, NX), lax.rem(x + 1, NX), lax.rem(x + 2, NX)
-    partner = (1 - zh) * PEERS + me8
 
     b_copy = pltpu.make_async_copy(b_hbm, b_raw, b_sem)
     b_copy.start()
 
+    partner = (1 - zh) * PEERS + me8
     barrier = pltpu.get_barrier_semaphore()
 
     def greet(r, c):
@@ -40,15 +40,19 @@
     greet(row, right)
     for d in range(1, PEERS):
         greet(zh * PEERS + lax.rem(me8 + d, PEERS), col)
-    greet(partner, col)
-
-    @pl.when(z > 0)
+
+    for d in (1, 2):
+        @pl.when(z >= d)
+        def _():
+            greet(row, col - d * NX)
+
+        @pl.when(z < NZ - d)
+        def _():
+            greet(row, col + d * NX)
+
+    @pl.when(zh == 0)
     def _():
-        greet(row, col - NX)
-
-    @pl.when(z < NZ - 1)
-    def _():
-        greet(row, col + NX)
+        greet(PEERS + me8, x)
 
     for k in range(n_chunks):
         own[k * NR : (k + 1) * NR, :] = amp_ref[:, k * LANES : (k + 1) * LANES]
@@ -56,16 +60,18 @@
         own[n_chunks * NR :, :] = jnp.zeros((rows - n_chunks * NR, LANES), jnp.float32)
     slabs[z, pl.ds(pl.multiple_of(x * rows, 8), rows), :] = own[...]
 
-    ends = jnp.where(z > 0, 1, 0) + jnp.where(z < NZ - 1, 1, 0)
-    pl.semaphore_wait(barrier, 2 + PEERS + ends)
+    near = 1 + PEERS + jnp.where((zh == 1) & (z == 0), NZ, 0)
+    for d in (1, 2):
+        near = near + jnp.where(z >= d, 1, 0) + jnp.where(z < NZ - d, 1, 0)
+    pl.semaphore_wait(barrier, near)
 
     def piece(zs, xs, p):
         return slabs.at[zs, pl.ds(pl.multiple_of(xs * rows + p * half, 8), half), :]
 
-    def z_copy(zs, p, up):
-        to = jnp.minimum(col + NX, NZ * NX - 1) if up else jnp.maximum(col - NX, 0)
-        ref = piece(zs, x, p)
-        return pltpu.make_async_remote_copy(ref, ref, z_send.at[up, zs, p], z_recv.at[zs, p],
+    def z_copy(zs, up, d):
+        to = jnp.minimum(col + d * NX, NZ * NX - 1) if up else jnp.maximum(col - d * NX, 0)
+        ref = slabs.at[zs, pl.ds(pl.multiple_of(x * rows, 8), rows), :]
+        return pltpu.make_async_remote_copy(ref, ref, z_send.at[up, d - 1, zs], z_recv.at[zs],
                                             device_id={"row": row, "col": to}, device_id_type=MESH)
 
     def x_copy(zs, p, to_right):
@@ -94,30 +100,36 @@
                                             p_recv.at[zs // PEERS, me8],
                                             device_id={"row": to, "col": col}, device_id_type=MESH)
 
-    pairs = jnp.minimum(z, NZ - 1 - z)
-
     def order(n):
-        near = (n + 1) // 2
-        near = jnp.where(lax.rem(n, 2) == 1, z - near, z + near)
-        far = jnp.where(z < NZ // 2, z + n - pairs, z - n + pairs)
-        return jnp.where(n <= 2 * pairs, near, far)
-
-    def z_start(zs, p, up):
-        @pl.when((z < NZ - 1) if up else (z > 0))
-        def _():
-            z_copy(zs, p, up).start()
+        low_first = jnp.where(n <= z, z - n, n)
+        high_first = jnp.where(n < NZ - z, z + n, NZ - 1 - n)
+        return jnp.where(zh == 1, low_first, high_first)
+
+    def z_start(zs, up):
+        for d in (2, 1):
+            @pl.when((z < NZ - d) if up else (z >= d))
+            def _():
+                z_copy(zs, up, d).start()
 
     def z_step(t):
-        for p in range(2):
-            @pl.when(z - t >= 0)
-            def _():
-                z_copy(z - t, p, 1).wait_recv()
-                z_start(z - t, p, 1)
-
-            @pl.when(z + t < NZ)
-            def _():
-                z_copy(z + t, p, 0).wait_recv()
-                z_start(z + t, p, 0)
+        for o in (2 * t, 2 * t - 1):
+            onward = lax.rem(o, 2) == 0
+
+            @pl.when(z - o >= 0)
+            def _():
+                z_copy(z - o, 1, 1).wait_recv()
+
+            @pl.when((z - o >= 0) & onward)
+            def _():
+                z_start(z - o, 1)
+
+            @pl.when(z + o < NZ)
+            def _():
+                z_copy(z + o, 0, 1).wait_recv()
+
+            @pl.when((z + o < NZ) & onward)
+            def _():
+                z_start(z + o, 0)
 
     def x_start(zs):
         x_copy(zs, 0, 1).start()
@@ -153,38 +165,6 @@
         def _():
             p_copy(zs).start()
 
-    for p in range(2):
-        z_start(z, p, 1)
-        z_start(z, p, 0)
-    x_start(z)
-
-    b_copy.wait()
-    depth = b_raw.shape[0]
-
-    @pl.loop(0, depth // 256)
-    def _(i):
-        at = pl.ds(pl.multiple_of(i * 256, 256), 256)
-        v = b_raw[at, :]
-        hi = v.astype(jnp.bfloat16)
-        b_hi[at, :] = hi
-        b_lo[at, :] = (v - hi.astype(jnp.float32)).astype(jnp.bfloat16)
-
-    @pl.loop(1, NZ + 2)
-    def _(t):
-        z_step(t)
-
-        @pl.when(t < NZ)
-        def _():
-            x_start(order(t))
-
-        @pl.when(t < NZ + 1)
-        def _():
-            x_forward(order(t - 1))
-
-        @pl.when(t >= 2)
-        def _():
-            finish(order(t - 2))
-
     def total(h):
         s = part[h * PEERS + me8]
         for d in range(1, PEERS):
@@ -194,10 +174,61 @@
             s = s + part_in[h, q]
         return jnp.concatenate([s[8 * i : 8 * i + NR, :] for i in range(NX)], axis=0)
 
-    cross[...] = total(1 - zh)
     c_copy = pltpu.make_async_remote_copy(cross, cross_in, c_send, c_recv,
                                           device_id={"row": partner, "col": col}, device_id_type=MESH)
-    c_copy.start()
+    theirs = (1 - zh) * PEERS + me8
+
+    told = jnp.maximum((z + 1) // 2, 1)
+    due = jnp.maximum((jnp.where(me8 <= z, z - me8, me8) + 7) // 2, told)
+
+    z_start(z, 1)
+    z_start(z, 0)
+    x_start(z)
+
+    b_copy.wait()
+    depth = b_raw.shape[0]
+
+    @pl.loop(0, depth // 256)
+    def _(i):
+        at = pl.ds(pl.multiple_of(i * 256, 256), 256)
+        v = b_raw[at, :]
+        hi = v.astype(jnp.bfloat16)
+        b_hi[at, :] = hi
+        b_lo[at, :] = (v - hi.astype(jnp.float32)).astype(jnp.bfloat16)
+
+    @pl.loop(1, NZ // 2 + 4)
+    def _(t):
+        z_step(t)
+        for n in (2 * t - 1, 2 * t):
+            @pl.when(n < NZ)
+            def _():
+                x_start(order(n))
+
+        for n in (2 * t - 3, 2 * t - 2):
+            @pl.when((n >= 0) & (n < NZ))
+            def _():
+                x_forward(order(n))
+
+        for n in (2 * t - 5, 2 * t - 4):
+            @pl.when((n >= 0) & (n < NZ))
+            def _():
+                finish(order(n))
+
+        @pl.when((zh == 1) & (t == told))
+        def _():
+            pl.semaphore_signal(here_sem, inc=1, device_id={"row": partner, "col": col}, device_id_type=MESH)
+
+        @pl.when((zh == 1) & (t == due))
+        def _():
+            cross[...] = total(1 - zh)
+            c_copy.start()
+
+    @pl.when(zh == 0)
+    def _():
+        pl.semaphore_wait(here_sem, 1)
+        cross[...] = total(1 - zh)
+        c_copy.start()
+
     mine = total(zh)
     c_copy.wait_recv()
     out_ref[...] = mine + cross_in[...]
@@ -205,15 +236,17 @@
 
     @pl.loop(0, NZ)
     def _(zs):
+        even = lax.rem(z + zs, 2) == 0
+        for d in (1, 2):
+            @pl.when((z < NZ - d) & (zs <= z) & even)
+            def _():
+                z_copy(zs, 1, d).wait_send()
+
+            @pl.when((z >= d) & (zs >= z) & even)
+            def _():
+                z_copy(zs, 0, d).wait_send()
+
         for p in range(2):
-            @pl.when((z < NZ - 1) & (zs <= z))
-            def _():
-                z_copy(zs, p, 1).wait_send()
-
-            @pl.when((z > 0) & (zs >= z))
-            def _():
-                z_copy(zs, p, 0).wait_send()
-
             for to_right in range(2):
                 x_copy(zs, p, to_right).wait_send()
         for to_right in range(2):
@@ -247,8 +280,8 @@
             pltpu.VMEM((NX * NR, width), f32),
             pltpu.VMEM((NX * NR, width), f32),
             dma,
-            dma((2, NZ, 2)),
-            dma((NZ, 2)),
+            dma((2, 2, NZ)),
+            dma((NZ,)),
             dma((2, NZ, 2)),
             dma((2, NZ, 2)),
             dma((2, NZ)),
@@ -257,9 +290,10 @@
             dma((2, PEERS)),
             dma,
             dma,
+            pltpu.SemaphoreType.REGULAR,
         ],
         compiler_params=pltpu.CompilerParams(
-            collective_id=0, has_side_effects=True, vmem_limit_bytes=40 * 1024 * 1024),
+            collective_id=0, has_side_effects=True, vmem_limit_bytes=60 * 1024 * 1024),
         cost_estimate=pl.CostEstimate(
             flops=6 * 512 * depth * width, bytes_accessed=4 * depth * width, transcendentals=0),
         name="ladder",

time: 98.6 us -> 74.1 us (0.75)
  the two profiles are of different devices: /device:TPU:8 before, /device:TPU:1016 now
where the time goes in v2:
time: 74.1 us; the launch traced here: 73.8 us
  Pallas kernels  72.3 us (98%)
  other arithmetic  1.43 us (2%)
    pallas_call x1, Pallas kernels, ladder_rows(): pl.pallas_call(functools.partial(kernel, n_chunks), out_shape=jax.ShapeDt...  72.3 us

profile of v2, /device:TPU:1016, one launch (start us, length us, event | category | flops | bytes accessed | tf_op | source)
XLA Modules:
  0.0 73.8 jit_solution(12564697674820197592)
XLA Ops:
  0.0 0.0 copy-start.1
  0.0 0.0 copy-start.2
  0.0 0.0 copy-start
  0.0 72.3 %ladder.1 = f32[20,256]{1,0:T(8,128)} custom-call(f32[5,2816]{1,0:T(8,128)} %amp_ref.1, f32[2816,256]{1,0:T(8,128)} %b_hbm.1), custom_call_target="tpu_custom_call" | custom-call | flops 2214592512 | bytes 2883584 | tf_op jit(solution)/shard_map/ladder/pallas_call | solution.py:266
  72.3 0.0 copy-done.1
  72.4 0.0 copy-done.2
  72.4 0.0 copy-done
  72.4 1.4 %subtract_divide_fusion = f32[20,256]{1,0:T(8,128)} fusion(f32[20,256]{1,0:T(8,128)S(1)} %copy-done, f32[20,256]{1,0:T(8,128)} %ladder.1, f32[256]{0:T(256)S(1)} %copy-done.1, f32[20]{0:T(128)S(1)} %copy-done.2), kind=kLoop, calls=%fused_computation | loop fusion | flops 20480 | bytes 62544 | tf_op jit(solution)/shard_map/div | solution.py:306
Async XLA Ops:
  0.0 72.3 %copy-start.1 = (f32[256]{0:T(256)S(1)}, f32[256]{0:T(256)}, u32[]{:S(2)}) copy-start(f32[256]{0:T(256)} %param.9) | copy-start | bytes 3076
  0.0 72.4 %copy-start.2 = (f32[20]{0:T(128)S(1)}, f32[20]{0:T(128)}, u32[]{:S(2)}) copy-start(f32[20]{0:T(128)} %param.8) | copy-start | bytes 244
  0.0 72.4 %copy-start = (f32[20,256]{1,0:T(8,128)S(1)}, f32[20,256]{1,0:T(8,128)}, u32[]{:S(2)}) copy-start(f32[20,256]{1,0:T(8,128)} %param.7) | copy-start | bytes 61444

commit v3 on v2

--- a/solution.py
+++ b/solution.py
@@ -12,11 +12,12 @@
 NZ = 16
 NR = 5
 LANES = 128
+LAST = 2
 PEERS = 8
 
 
-def kernel(n_chunks, amp_ref, b_hbm, out_ref, own, slabs, b_raw, b_hi, b_lo, lhs, part, part_in, cross, cross_in,
-           b_sem, z_send, z_recv, x_send, x_recv, f_send, f_recv, p_send, p_recv, c_send, c_recv, here_sem):
+def kernel(n_chunks, amp_hbm, b_hbm, out_ref, amp, own, slabs, b_raw, b_hi, b_lo, lhs, part, part_in, cross, cross_in,
+           a_sem, b_sem, z_send, z_recv, x_send, x_recv, f_send, f_recv, p_send, p_recv, c_send, c_recv, here_sem):
     rows = own.shape[0]
     half = rows // 2
     row = lax.axis_index("row")
@@ -27,6 +28,8 @@
     left = z * NX + lax.rem(x + NX - 1, NX)
     x_left, x_right, x_far = lax.rem(x + 3, NX), lax.rem(x + 1, NX), lax.rem(x + 2, NX)
 
+    a_copy = pltpu.make_async_copy(amp_hbm, amp, a_sem)
+    a_copy.start()
     b_copy = pltpu.make_async_copy(b_hbm, b_raw, b_sem)
     b_copy.start()
 
@@ -54,8 +57,9 @@
     def _():
         greet(PEERS + me8, x)
 
+    a_copy.wait()
     for k in range(n_chunks):
-        own[k * NR : (k + 1) * NR, :] = amp_ref[:, k * LANES : (k + 1) * LANES]
+        own[k * NR : (k + 1) * NR, :] = amp[:, k * LANES : (k + 1) * LANES]
     if n_chunks * NR < rows:
         own[n_chunks * NR :, :] = jnp.zeros((rows - n_chunks * NR, LANES), jnp.float32)
     slabs[z, pl.ds(pl.multiple_of(x * rows, 8), rows), :] = own[...]
@@ -68,11 +72,19 @@
     def piece(zs, xs, p):
         return slabs.at[zs, pl.ds(pl.multiple_of(xs * rows + p * half, 8), half), :]
 
-    def z_copy(zs, up, d):
+    def z_device(up, d):
         to = jnp.minimum(col + d * NX, NZ * NX - 1) if up else jnp.maximum(col - d * NX, 0)
+        return {"row": row, "col": to}
+
+    def z_far(zs, up, p):
+        ref = piece(zs, x, p)
+        return pltpu.make_async_remote_copy(ref, ref, z_send.at[up, p, zs], z_recv.at[zs, p],
+                                            device_id=z_device(up, 2), device_id_type=MESH)
+
+    def z_near(zs, up):
         ref = slabs.at[zs, pl.ds(pl.multiple_of(x * rows, 8), rows), :]
-        return pltpu.make_async_remote_copy(ref, ref, z_send.at[up, d - 1, zs], z_recv.at[zs],
-                                            device_id={"row": row, "col": to}, device_id_type=MESH)
+        return pltpu.make_async_remote_copy(ref, ref, z_send.at[up, 2, zs], z_recv.at[zs, 0],
+                                            device_id=z_device(up, 1), device_id_type=MESH)
 
     def x_copy(zs, p, to_right):
         ref = piece(zs, x, p)
@@ -90,6 +102,11 @@
                                             device_id={"row": row, "col": right if to_right else left},
                                             device_id_type=MESH)
 
+    def far_copy(zs, to_right):
+        ref = piece(zs, x, 1 - to_right)
+        return pltpu.make_async_remote_copy(ref, ref, f_send.at[to_right, zs], f_recv.at[to_right, zs],
+                                            device_id={"row": row, "col": z * NX + x_far}, device_id_type=MESH)
+
     def f_arrival(zs, to_right):
         ref = piece(zs, x_far, 1 - to_right)
         return pltpu.make_async_copy(ref, ref, f_recv.at[to_right, zs])
@@ -105,43 +122,67 @@
         high_first = jnp.where(n < NZ - z, z + n, NZ - 1 - n)
         return jnp.where(zh == 1, low_first, high_first)
 
-    def z_start(zs, up):
-        for d in (2, 1):
-            @pl.when((z < NZ - d) if up else (z >= d))
-            def _():
-                z_copy(zs, up, d).start()
+    def far_start(zs, up, p):
+        @pl.when((z < NZ - 2) if up else (z >= 2))
+        def _():
+            z_far(zs, up, p).start()
+
+    def near_start(zs, up):
+        @pl.when((z < NZ - 1) if up else (z >= 1))
+        def _():
+            z_near(zs, up).start()
 
     def z_step(t):
-        for o in (2 * t, 2 * t - 1):
-            onward = lax.rem(o, 2) == 0
-
-            @pl.when(z - o >= 0)
-            def _():
-                z_copy(z - o, 1, 1).wait_recv()
-
-            @pl.when((z - o >= 0) & onward)
-            def _():
-                z_start(z - o, 1)
-
-            @pl.when(z + o < NZ)
-            def _():
-                z_copy(z + o, 0, 1).wait_recv()
-
-            @pl.when((z + o < NZ) & onward)
-            def _():
-                z_start(z + o, 0)
-
-    def x_start(zs):
+        below, above = z - 2 * t, z + 2 * t
+        for p in range(2):
+            @pl.when(below >= 0)
+            def _():
+                z_far(below, 1, p).wait_recv()
+                far_start(below, 1, p)
+
+            @pl.when(above < NZ)
+            def _():
+                z_far(above, 0, p).wait_recv()
+                far_start(above, 0, p)
+
+        @pl.when(below >= 0)
+        def _():
+            near_start(below, 1)
+
+        @pl.when(above < NZ)
+        def _():
+            near_start(above, 0)
+
+        @pl.when(below + 1 >= 0)
+        def _():
+            z_near(below + 1, 1).wait_recv()
+
+        @pl.when(above - 1 < NZ)
+        def _():
+            z_near(above - 1, 0).wait_recv()
+
+    def x_start(n):
+        zs = order(n)
+
+        @pl.when(n >= NZ - LAST)
+        def _():
+            far_copy(zs, 1).start()
+            far_copy(zs, 0).start()
+
         x_copy(zs, 0, 1).start()
         x_copy(zs, 1, 0).start()
         x_copy(zs, 1, 1).start()
         x_copy(zs, 0, 0).start()
 
-    def x_forward(zs):
+    def x_forward(n):
+        zs = order(n)
         x_arrival(zs, 0, 1).wait()
-        f_copy(zs, 1).start()
         x_arrival(zs, 1, 0).wait()
-        f_copy(zs, 0).start()
+
+        @pl.when(n < NZ - LAST)
+        def _():
+            f_copy(zs, 1).start()
+            f_copy(zs, 0).start()
 
     def finish(zs):
         x_arrival(zs, 1, 1).wait()
@@ -176,14 +217,18 @@
 
     c_copy = pltpu.make_async_remote_copy(cross, cross_in, c_send, c_recv,
                                           device_id={"row": partner, "col": col}, device_id_type=MESH)
-    theirs = (1 - zh) * PEERS + me8
 
     told = jnp.maximum((z + 1) // 2, 1)
-    due = jnp.maximum((jnp.where(me8 <= z, z - me8, me8) + 7) // 2, told)
-
-    z_start(z, 1)
-    z_start(z, 0)
-    x_start(z)
+    high = PEERS + me8
+    turn = jnp.where(zh == 1, jnp.where(me8 <= z, z - me8, me8), jnp.where(high >= z, high - z, NZ - 1 - high))
+    due = jnp.maximum((turn + 9) // 2, jnp.where(zh == 1, told, NZ // 2 + z // 5))
+
+    for p in range(2):
+        far_start(z, 1, p)
+        far_start(z, 0, p)
+    near_start(z, 1)
+    near_start(z, 0)
+    x_start(0)
 
     b_copy.wait()
     depth = b_raw.shape[0]
@@ -196,55 +241,50 @@
         b_hi[at, :] = hi
         b_lo[at, :] = (v - hi.astype(jnp.float32)).astype(jnp.bfloat16)
 
-    @pl.loop(1, NZ // 2 + 4)
+    @pl.loop(1, NZ // 2 + 5)
     def _(t):
         z_step(t)
         for n in (2 * t - 1, 2 * t):
             @pl.when(n < NZ)
             def _():
-                x_start(order(n))
+                x_start(n)
+
+        for n in (2 * t - 7, 2 * t - 6):
+            @pl.when((n >= 0) & (n < NZ))
+            def _():
+                finish(order(n))
 
         for n in (2 * t - 3, 2 * t - 2):
             @pl.when((n >= 0) & (n < NZ))
             def _():
-                x_forward(order(n))
-
-        for n in (2 * t - 5, 2 * t - 4):
-            @pl.when((n >= 0) & (n < NZ))
-            def _():
-                finish(order(n))
+                x_forward(n)
 
         @pl.when((zh == 1) & (t == told))
         def _():
             pl.semaphore_signal(here_sem, inc=1, device_id={"row": partner, "col": col}, device_id_type=MESH)
 
-        @pl.when((zh == 1) & (t == due))
+        @pl.when((zh == 0) & (t == due))
+        def _():
+            pl.semaphore_wait(here_sem, 1)
+
+        @pl.when(t == due)
         def _():
             cross[...] = total(1 - zh)
             c_copy.start()
-
-    @pl.when(zh == 0)
-    def _():
-        pl.semaphore_wait(here_sem, 1)
-        cross[...] = total(1 - zh)
-        c_copy.start()
-
-    mine = total(zh)
-    c_copy.wait_recv()
-    out_ref[...] = mine + cross_in[...]
-    c_copy.wait_send()
 
     @pl.loop(0, NZ)
     def _(zs):
         even = lax.rem(z + zs, 2) == 0
-        for d in (1, 2):
-            @pl.when((z < NZ - d) & (zs <= z) & even)
-            def _():
-                z_copy(zs, 1, d).wait_send()
-
-            @pl.when((z >= d) & (zs >= z) & even)
-            def _():
-                z_copy(zs, 0, d).wait_send()
+        for up in range(2):
+            passed = even & ((zs <= z) if up else (zs >= z))
+            for p in range(2):
+                @pl.when(passed & ((z < NZ - 2) if up else (z >= 2)))
+                def _():
+                    z_far(zs, up, p).wait_send()
+
+            @pl.when(passed & ((z < NZ - 1) if up else (z >= 1)))
+            def _():
+                z_near(zs, up).wait_send()
 
         for p in range(2):
             for to_right in range(2):
@@ -255,6 +295,11 @@
         @pl.when(lax.rem(zs, PEERS) != me8)
         def _():
             p_copy(zs).wait_send()
+
+    mine = total(zh)
+    c_copy.wait_recv()
+    out_ref[...] = mine + cross_in[...]
+    c_copy.wait_send()
 
 
 def ladder_rows(amplitudes, integrals):
@@ -266,9 +311,10 @@
     return pl.pallas_call(
         functools.partial(kernel, n_chunks),
         out_shape=jax.ShapeDtypeStruct((NX * NR, width), f32),
-        in_specs=[pl.BlockSpec(memory_space=pltpu.VMEM), pl.BlockSpec(memory_space=pl.ANY)],
+        in_specs=[pl.BlockSpec(memory_space=pl.ANY)] * 2,
         out_specs=pl.BlockSpec(memory_space=pltpu.VMEM),
         scratch_shapes=[
+            pltpu.VMEM(amplitudes.shape, f32),
             pltpu.VMEM((rows, LANES), f32),
             pltpu.VMEM((NZ, NX * rows + 8, LANES), f32),
             pltpu.VMEM((depth, width), f32),
@@ -280,8 +326,9 @@
             pltpu.VMEM((NX * NR, width), f32),
             pltpu.VMEM((NX * NR, width), f32),
             dma,
-            dma((2, 2, NZ)),
-            dma((NZ,)),
+            dma,
+            dma((2, 3, NZ)),
+            dma((NZ, 2)),
             dma((2, NZ, 2)),
             dma((2, NZ, 2)),
             dma((2, NZ)),

time: 74.1 us -> 71.4 us (0.964)
  the two profiles are of different devices: /device:TPU:1016 before, /device:TPU:25 now
where the time goes in v3:
time: 71.4 us; the launch traced here: 71.1 us
  Pallas kernels  69.6 us (97%)
  other arithmetic  1.43 us (2%)
    pallas_call x1, Pallas kernels, ladder_rows(): pl.pallas_call(functools.partial(kernel, n_chunks), out_shape=jax.ShapeDt...  69.6 us

profile of v3, /device:TPU:25, one launch (start us, length us, event | category | flops | bytes accessed | tf_op | source)
XLA Modules:
  0.0 71.1 jit_solution(8994143060457844004)
XLA Ops:
  0.0 0.0 copy-start.1
  0.0 0.0 copy-start.2
  0.0 0.0 copy-start
  0.0 69.6 %ladder.1 = f32[20,256]{1,0:T(8,128)} custom-call(f32[5,2816]{1,0:T(8,128)} %amp_hbm.1, f32[2816,256]{1,0:T(8,128)} %b_hbm.1), custom_call_target="tpu_custom_call" | custom-call | flops 2214592512 | bytes 2883584 | tf_op jit(solution)/shard_map/ladder/pallas_call | solution.py:311
  69.6 0.0 copy-done.1
  69.6 0.0 copy-done.2
  69.7 0.0 copy-done
  69.7 1.4 %subtract_divide_fusion = f32[20,256]{1,0:T(8,128)} fusion(f32[20,256]{1,0:T(8,128)S(1)} %copy-done, f32[20,256]{1,0:T(8,128)} %ladder.1, f32[256]{0:T(256)S(1)} %copy-done.1, f32[20]{0:T(128)S(1)} %copy-done.2), kind=kLoop, calls=%fused_computation | loop fusion | flops 20480 | bytes 62544 | tf_op jit(solution)/shard_map/div | solution.py:353
Async XLA Ops:
  0.0 69.6 %copy-start.1 = (f32[256]{0:T(256)S(1)}, f32[256]{0:T(256)}, u32[]{:S(2)}) copy-start(f32[256]{0:T(256)} %param.9) | copy-start | bytes 3076
  0.0 69.6 %copy-start.2 = (f32[20]{0:T(128)S(1)}, f32[20]{0:T(128)}, u32[]{:S(2)}) copy-start(f32[20]{0:T(128)} %param.8) | copy-start | bytes 244
  0.0 69.6 %copy-start = (f32[20,256]{1,0:T(8,128)S(1)}, f32[20,256]{1,0:T(8,128)}, u32[]{:S(2)}) copy-start(f32[20,256]{1,0:T(8,128)} %param.7) | copy-start | bytes 61444

commit v4 on v3

--- a/solution.py
+++ b/solution.py
@@ -12,7 +12,8 @@
 NZ = 16
 NR = 5
 LANES = 128
-LAST = 2
+HUB = 2
+LAST = 4
 PEERS = 8
 
 
@@ -55,7 +56,7 @@
 
     @pl.when(zh == 0)
     def _():
-        greet(PEERS + me8, x)
+        greet(PEERS + me8, jnp.minimum(z, HUB) * NX + x)
 
     a_copy.wait()
     for k in range(n_chunks):
@@ -64,7 +65,7 @@
         own[n_chunks * NR :, :] = jnp.zeros((rows - n_chunks * NR, LANES), jnp.float32)
     slabs[z, pl.ds(pl.multiple_of(x * rows, 8), rows), :] = own[...]
 
-    near = 1 + PEERS + jnp.where((zh == 1) & (z == 0), NZ, 0)
+    near = 1 + PEERS + jnp.where(zh == 1, jnp.where(z < HUB, 1, jnp.where(z == HUB, NZ - HUB, 0)), 0)
     for d in (1, 2):
         near = near + jnp.where(z >= d, 1, 0) + jnp.where(z < NZ - d, 1, 0)
     pl.semaphore_wait(barrier, near)
@@ -218,10 +219,10 @@
     c_copy = pltpu.make_async_remote_copy(cross, cross_in, c_send, c_recv,
                                           device_id={"row": partner, "col": col}, device_id_type=MESH)
 
-    told = jnp.maximum((z + 1) // 2, 1)
+    told = jnp.maximum((z + 1 - HUB) // 2, 1)
     high = PEERS + me8
     turn = jnp.where(zh == 1, jnp.where(me8 <= z, z - me8, me8), jnp.where(high >= z, high - z, NZ - 1 - high))
-    due = jnp.maximum((turn + 9) // 2, jnp.where(zh == 1, told, NZ // 2 + z // 5))
+    due = jnp.maximum((turn + 7) // 2, jnp.where(zh == 1, told, (25 + 4 * told - z) // 4 + 1))
 
     for p in range(2):
         far_start(z, 1, p)
@@ -241,7 +242,7 @@
         b_hi[at, :] = hi
         b_lo[at, :] = (v - hi.astype(jnp.float32)).astype(jnp.bfloat16)
 
-    @pl.loop(1, NZ // 2 + 5)
+    @pl.loop(1, NZ // 2 + 4)
     def _(t):
         z_step(t)
         for n in (2 * t - 1, 2 * t):
@@ -249,15 +250,15 @@
             def _():
                 x_start(n)
 
-        for n in (2 * t - 7, 2 * t - 6):
-            @pl.when((n >= 0) & (n < NZ))
-            def _():
-                finish(order(n))
-
         for n in (2 * t - 3, 2 * t - 2):
             @pl.when((n >= 0) & (n < NZ))
             def _():
                 x_forward(n)
+
+        for n in (2 * t - 5, 2 * t - 4):
+            @pl.when((n >= 0) & (n < NZ))
+            def _():
+                finish(order(n))
 
         @pl.when((zh == 1) & (t == told))
         def _():

time: 71.4 us -> 72.2 us (1.011)
  the two profiles are of different devices: /device:TPU:25 before, /device:TPU:352 now
where the time goes in v4:
time: 72.2 us; the launch traced here: 72 us
  Pallas kernels  70.5 us (98%)
  other arithmetic  1.43 us (2%)
    pallas_call x1, Pallas kernels, ladder_rows(): pl.pallas_call(functools.partial(kernel, n_chunks), out_shape=jax.ShapeDt...  70.5 us

profile of v4, /device:TPU:352, one launch (start us, length us, event | category | flops | bytes accessed | tf_op | source)
XLA Modules:
  0.0 72.0 jit_solution(7549618378684210248)
XLA Ops:
  0.0 0.0 copy-start.1
  0.0 0.0 copy-start.2
  0.0 0.0 copy-start
  0.0 70.5 %ladder.1 = f32[20,256]{1,0:T(8,128)} custom-call(f32[5,2816]{1,0:T(8,128)} %amp_hbm.1, f32[2816,256]{1,0:T(8,128)} %b_hbm.1), custom_call_target="tpu_custom_call" | custom-call | flops 2214592512 | bytes 2883584 | tf_op jit(solution)/shard_map/ladder/pallas_call | solution.py:312
  70.5 0.0 copy-done.1
  70.5 0.0 copy-done.2
  70.5 0.0 copy-done
  70.6 1.4 %subtract_divide_fusion = f32[20,256]{1,0:T(8,128)} fusion(f32[20,256]{1,0:T(8,128)S(1)} %copy-done, f32[20,256]{1,0:T(8,128)} %ladder.1, f32[256]{0:T(256)S(1)} %copy-done.1, f32[20]{0:T(128)S(1)} %copy-done.2), kind=kLoop, calls=%fused_computation | loop fusion | flops 20480 | bytes 62544 | tf_op jit(solution)/shard_map/div | solution.py:354
Async XLA Ops:
  0.0 70.5 %copy-start.1 = (f32[256]{0:T(256)S(1)}, f32[256]{0:T(256)}, u32[]{:S(2)}) copy-start(f32[256]{0:T(256)} %param.9) | copy-start | bytes 3076
  0.0 70.5 %copy-start.2 = (f32[20]{0:T(128)S(1)}, f32[20]{0:T(128)}, u32[]{:S(2)}) copy-start(f32[20]{0:T(128)} %param.8) | copy-start | bytes 244
  0.0 70.5 %copy-start = (f32[20,256]{1,0:T(8,128)S(1)}, f32[20,256]{1,0:T(8,128)}, u32[]{:S(2)}) copy-start(f32[20,256]{1,0:T(8,128)} %param.7) | copy-start | bytes 61444
